TPU v7x, 32 devices: a whole 2x2x4 slice. The times are simulated.
32 devices in a mesh: pairs: 8 (over z, x), own: 4 (over y, core).
Axes of the slice: x: 2, y: 2, z: 4, core: 2. Of those that a mesh axis runs over, the one named last changes fastest.
Arguments:
- amplitudes: bfloat16 [512, 4, 4096], P(('pairs', 'own')), may hold values from -6 to 6
- integrals: bfloat16 [4, 4096, 4, 4096], P('own', None, None, 'pairs'), may hold values from -0.046875 to 0.046875
- owner: int32 [4], replicated, may hold values from 0 to 3, each once
- amp_mask: int32 [512, 4], P(('pairs', 'own')), may hold values 0 or 1
- int_mask: int32 [4, 4], replicated, may hold values from 0 to 1, as said below
- out_mask: int32 [4], replicated, may hold values from 0 to 1, as said below
Outputs:
- ladder: bfloat16 [512, 4, 4096], P(('pairs', 'own'))
Inputs may be any that keep to these rules, and one draw needn't show every extreme that they name: `int_mask`: every column has a 1 in some row. `out_mask`: at least one entry is 1. `owner`: each slot holds exactly one piece.
All inputs are finite; a program needn't handle non-finite values. No bound on the sum of `amp_mask` on one device may be relied on, other than what follows from the above.
Results may differ from a plain program's by a relative error of at most 0.001.
Values may be sent and summed in bfloat16 or wider, within the bound.
A program may use at most 128 MiB of HBM per device.

v0:
```python
import jax
import jax.numpy as jnp
from jax import lax
from jax.sharding import PartitionSpec as P


def local(amplitudes, integrals, owner, amp_mask, int_mask, out_mask):
    own_count = lax.axis_size("own")
    pairs_count = lax.axis_size("pairs")
    slab = integrals[0]
    piece_rows, tile_count, col_count = slab.shape
    pair_rows, panel_count, tile_pair = amplitudes.shape
    rows = pair_rows * pairs_count * own_count
    slots = jnp.arange(own_count, dtype=jnp.int32)
    piece_of = jnp.sum(jnp.where(owner[:, None] == slots[None, :], slots[:, None], 0), axis=0)
    my_piece = piece_of[lax.axis_index("own")]
    my_tile = my_piece * piece_rows // tile_pair
    masked_t = amplitudes * amp_mask.astype(amplitudes.dtype)[:, :, None]
    pieces = masked_t.reshape(pair_rows, own_count, piece_rows)
    ordered = jnp.stack(
        [lax.dynamic_index_in_dim(pieces, piece_of[slot], 1, keepdims=False) for slot in range(own_count)], axis=1
    )
    mine = lax.all_to_all(ordered, "own", split_axis=1, concat_axis=0, tiled=True)
    gathered = lax.all_gather(mine.reshape(own_count * pair_rows, piece_rows), "pairs", axis=0, tiled=True)
    summed = jnp.dot(gathered, slab.reshape(piece_rows, tile_count * col_count), preferred_element_type=jnp.float32)
    keep = (int_mask[my_tile] * out_mask).astype(jnp.float32)
    part = summed.reshape(pairs_count, own_count, pair_rows, tile_count, col_count) * keep[:, None]
    total = lax.psum_scatter(part, "own", scatter_dimension=1, tiled=False)
    rounded = total.astype(jnp.bfloat16)
    moved = lax.all_to_all(rounded, "pairs", split_axis=0, concat_axis=3, tiled=True)
    return moved[0]


def solution(mesh):
    return jax.shard_map(
        local,
        mesh=mesh,
        in_specs=(
            P(("pairs", "own"), None, None),
            P("own", None, None, "pairs"),
            P(),
            P(("pairs", "own"), None),
            P(),
            P(),
        ),
        out_specs=P(("pairs", "own"), None, None),
        check_vma=False,
    )
```

profile of v0, /device:TPU:0, one launch (start us, length us, event | category | flops | bytes accessed | tf_op | source)
XLA Modules:
  0.0 224.0 jit_solution(15439697620026197893)
XLA Ops:
  6.5 0.0 all-gather.2.cloned.1.call-start
  6.5 0.7 select_reduce_fusion
  7.3 0.7 fusion.4
  12.9 0.7 convert_element_type.12
  16.1 1.6 copy_multiply_fusion
  17.8 0.1 pad_maximum_fusion
  17.9 13.0 %all_to_all.30 = bf16[16,4,4096]{2,0,1:T(8,128)(2,1)} all-to-all(bf16[16,4,4096]{2,0,1:T(8,128)(2,1)S(1)} %pad_maximum_fusion), channel_id=1, replica_groups=mesh['pairs'=8,'own'=4] {'own'}, dimensions={1} | all-to-all | bytes 1048576 | tf_op jit(solution)/shard_map/all_to_all | solution.py:23
  30.9 0.0 all-gather.2.cloned.1.call-update
  31.6 17.0 %copy.27 = bf16[512,8,4,512]{3,1,2,0:T(8,128)(2,1)} copy(bf16[512,8,4,512]{3,2,1,0:T(4,128)(2,1)} %bitcast.50) | data formatting | bytes 33554432
  48.5 0.0 copy-start.1
  48.5 0.0 copy-start
  48.5 20.9 %copy.18 = bf16[2048,4096]{1,0:T(8,128)(2,1)} copy(bf16[2048,4096]{0,1:T(8,128)(2,1)} %bitcast.49) | data formatting | bytes 33554432 | tf_op jit(solution)/shard_map/dot_general | solution.py:25
  69.4 0.0 copy-done.1
  69.5 0.6 dynamic-slice
  70.0 0.0 copy-done
  70.0 0.7 fusion.3
  70.7 34.4 %all-gather.2.cloned.1.call-done = bf16[512,4096]{1,0:T(8,128)(2,1)} async-done(((bf16[64,4096]{1,0:T(8,128)(2,1)}), bf16[512,4096]{1,0:T(8,128)(2,1)}) %all-gather.2.cloned.1.call-update) | async-done | bytes 4194320 | tf_op jit(solution)/shard_map/all_gather | solution.py:24
  105.1 15.0 %convolution_multiply_fusion = f32[8,4,16,4,512]{4,2,3,1,0:T(8,128)} fusion(bf16[8,4,16,4096,1]{3,2,4,1,0:T(8,128)(2,1)} %bitcast.54, bf16[4,512,4096,1,1]{2,1,0,4,3:T(8,128)(2,1)} %bitcast.51, f32[4]{0:T(128)S(1)} %fusion.3), kind=kOutput, calls=%fused_computation | convolution fusion | flops 8590983168 | bytes 25165840 | tf_op jit(solution)/shard_map/dot_general | solution.py:25
  120.2 75.9 %all-reduce.2 = bf16[8,4,16,4,512]{4,2,3,1,0:T(8,128)(2,1)S(1)} all-reduce(f32[8,4,16,4,512]{4,2,3,1,0:T(8,128)} %convolution_multiply_fusion), channel_id=2, replica_groups=mesh['pairs'=8,'own'=4] {'own'}, use_global_device_ids=true, to_apply=%region_1.2.clone | all-reduce | flops 1048576 | bytes 6291456
  196.1 0.7 fusion
  196.7 18.9 %all_to_all.31 = bf16[8,16,4,512]{3,1,2,0:T(8,128)(2,1)S(1)} all-to-all(bf16[8,16,4,512]{3,1,2,0:T(8,128)(2,1)S(1)} %fusion), channel_id=1, replica_groups=mesh['pairs'=8,'own'=4] {'pairs'}, dimensions={0} | all-to-all | bytes 1048576 | tf_op jit(solution)/shard_map/all_to_all | solution.py:30
  215.7 0.3 copy.23
  215.9 1.2 reshape.17
  (1 shorter events, 0.0 us)
Async XLA Ops:
  6.5 98.6 %all-gather.2.cloned.1.call-start = ((), (), s32[]{:S(2)}) async-start(), calls=%async_computation.2 | async-start | bytes 4718592 | tf_op jit(solution)/shard_map/all_gather | solution.py:24
  48.5 20.9 %copy-start.1 = (u32[32]{0:T(128)S(1)}, u32[32]{0:T(128)}, u32[]{:S(2)}) copy-start(u32[32]{0:T(128)} %constant.40) | copy-start | bytes 388
  48.5 21.5 %copy-start = (s32[4]{0:T(128)S(1)}, s32[4]{0:T(128)}, u32[]{:S(2)}) copy-start(s32[4]{0:T(128)} %param.11) | copy-start | bytes 52
Sparse Core Ops, SparseCore 0:
  31.0 74.0 all-gather.1
where the time goes:
time: 225 us; the launch traced here: 224 us
  blocking collectives  108 us (48%)
  local copies, waits for them, and re-layouts  41.3 us (18%)
  waiting for transfers between devices  34.4 us (15%)
  between operations  21.6 us (10%)
  matrix products  15 us (7%)
  other arithmetic  3.81 us (2%)
    unnamed x1, blocking collectives  75.9 us
    all_gather x1, waiting for transfers between devices, local(): lax.all_gather(mine.reshape(own_count * pair_rows, piece_rows), 'pairs',...  34.4 us
    dot_general x1, local copies, waits for them, and re-layouts, local(): jnp.dot(gathered, slab.reshape(piece_rows, tile_count * col_count), prefe...  20.9 us
    all_to_all x1, blocking collectives, local(): lax.all_to_all(rounded, 'pairs', split_axis=0, concat_axis=3, tiled=True)  18.9 us
    unnamed x6, local copies, waits for them, and re-layouts  17.6 us
    dot_general x1, matrix products, local(): jnp.dot(gathered, slab.reshape(piece_rows, tile_count * col_count), prefe...  15 us
    all_to_all x1, blocking collectives, local(): lax.all_to_all(ordered, 'own', split_axis=1, concat_axis=0, tiled=True)  13 us
  transfers between devices with their start and end apart: 1, of which 1 were waited for; matrix products, arithmetic and copies ran while one was open for 17% of the time, Pallas kernels for 0%

commit v1 on v0

v1 whole, which is shorter than its diff:
```python
import functools
import math

import jax
import jax.numpy as jnp
from jax import lax
from jax.experimental import pallas as pl
from jax.experimental.pallas import tpu as pltpu
from jax.sharding import PartitionSpec as P

MESH = pl.DeviceIdType.MESH
CHUNK = 256


def kernel(sizes, t_ref, v_ref, keep_ref, out_ref, tbuf, vbuf, stage, part, core_in, side_in, done,
           v_sem, own_send, own_recv, z_send, z_recv, x_send, x_recv, c_send, c_recv, y_send, y_recv, o_send, o_recv):
    Z, X, Y, K, N, cols, step_cols = sizes
    O, PAIRS = 2 * Y, Z * X
    pair, own = lax.axis_index("pairs"), lax.axis_index("own")
    z, x = pair // X, pair % X
    y, c = own // 2, own % 2

    def own_at(fy, fc):
        return ((y + Y + fy) % Y) * 2 + (c + 2 + fc) % 2

    def pair_at(d, e):
        return ((z + Z + d) % Z) * X + (x + X + e) % X

    def remote(src, dst, send, recv, device):
        return pltpu.make_async_remote_copy(
            src_ref=src, dst_ref=dst, send_sem=send, recv_sem=recv, device_id=device, device_id_type=MESH
        )

    barrier = pltpu.get_barrier_semaphore()
    for f in range(1, O):
        pl.semaphore_signal(barrier, inc=1, device_id={"own": (own + f) % O}, device_id_type=MESH)
    for g in range(1, PAIRS):
        pl.semaphore_signal(barrier, inc=1, device_id={"pairs": (pair + g) % PAIRS}, device_id_type=MESH)

    chunks = K // CHUNK

    def load(i, slot):
        rows = pl.ds(pl.multiple_of(i * CHUNK, CHUNK), CHUNK)
        return pltpu.make_async_copy(v_ref.at[rows], stage.at[slot], v_sem.at[slot])

    load(0, 0).start()
    load(1, 1).start()
    pl.semaphore_wait(barrier, O - 1 + PAIRS - 1)

    own_copies = []
    for f in range(1, O):
        fy, fc = f // 2, f % 2
        to = own_at(fy, fc)
        copy = remote(t_ref.at[to], tbuf.at[0, 0, fc, fy], own_send.at[f], own_recv.at[f], {"own": to})
        copy.start()
        own_copies.append(copy)
    tbuf[0, 0, 0, 0] = t_ref[own]
    for copy in own_copies:
        copy.wait_recv()

    z_copies = {}
    for d in range(1, Z):
        z_copies[d] = remote(tbuf.at[0, 0], tbuf.at[d, 0], z_send.at[d], z_recv.at[d], {"pairs": pair_at(d, 0)})
        z_copies[d].start()
    x_copies = {}

    def forward(d):
        for e in range(1, X):
            x_copies[d, e] = remote(
                tbuf.at[d, 0], tbuf.at[d, e], x_send.at[d, e], x_recv.at[d, e], {"pairs": pair_at(0, e)}
            )
            x_copies[d, e].start()

    forward(0)

    def flatten(first, last):
        @pl.loop(first // 2, last // 2)
        def _(pairno):
            for slot in range(2):
                i = pairno * 2 + slot
                load(i, slot).wait()
                rows = pl.ds(pl.multiple_of(i * CHUNK, CHUNK), CHUNK)
                vbuf[rows, :] = stage[slot].reshape(CHUNK, N)

                @pl.when(i + 2 < chunks)
                def _():
                    load(i + 2, slot).start()

    flatten(0, chunks)

    c_copies, y_copies, o_copies = {}, {}, []

    def multiply(d):
        rows = tbuf.at[d]

        @pl.loop(0, N // step_cols)
        def _(n):
            at = pl.ds(pl.multiple_of(n * step_cols, step_cols), step_cols)
            a = rows[...].reshape(X * O * 16, K)
            product = jnp.dot(a, vbuf[:, at], preferred_element_type=jnp.float32)
            scale = keep_ref[n * step_cols // cols]
            part[d, :, :, :, :, at] = (product * scale).reshape(X, 2, Y, 16, step_cols)

        c_copies[d] = remote(part.at[d, :, 1], core_in.at[d], c_send.at[d], c_recv.at[d], {"own": own_at(0, 1)})
        c_copies[d].start()

    def add_core(d):
        c_copies[d].wait_recv()
        for e in range(X):
            for fy in range(Y):
                part[d, e, 0, fy] = part[d, e, 0, fy] + core_in[d, e, fy]
        for fy in range(1, Y):
            y_copies[d, fy] = remote(
                part.at[d, :, 0, fy], side_in.at[d, fy], y_send.at[d, fy], y_recv.at[d, fy], {"own": own_at(-fy, 0)}
            )
            y_copies[d, fy].start()

    def add_side(d):
        for fy in range(1, Y):
            y_copies[d, fy].wait_recv()
        for e in range(X):
            total = part[d, e, 0, 0]
            for fy in range(1, Y):
                total = total + side_in[d, fy, e]
            rounded = total.astype(jnp.bfloat16)
            if d == 0 and e == 0:
                out_ref[pair] = rounded
            else:
                done[d, e] = rounded
                copy = remote(done.at[d, e], out_ref.at[pair], o_send.at[d, e], o_recv.at[d, e], {"pairs": pair_at(-d, -e)})
                copy.start()
                o_copies.append(copy)

    for d in range(Z):
        if d + 1 < Z:
            z_copies[d + 1].wait_recv()
            forward(d + 1)
        for e in range(1, X):
            x_copies[d, e].wait_recv()
        multiply(d)
        if d >= 1:
            add_core(d - 1)
        if d >= 2:
            add_side(d - 2)
    add_core(Z - 1)
    if Z >= 2:
        add_side(Z - 2)
    add_side(Z - 1)
    for copy in o_copies:
        copy.wait_recv()
    for group in (own_copies, z_copies.values(), x_copies.values(), c_copies.values(), y_copies.values(), o_copies):
        for copy in group:
            copy.wait_send()


def local(amplitudes, integrals, owner, amp_mask, int_mask, out_mask):
    own_count = lax.axis_size("own")
    pairs_count = lax.axis_size("pairs")
    slab = integrals[0]
    piece_rows, tile_count, col_count = slab.shape
    pair_rows, panel_count, tile_pair = amplitudes.shape
    width = tile_count * col_count
    X = math.isqrt(pairs_count // 2)
    Z = pairs_count // X
    Y = own_count // 2
    slots = jnp.arange(own_count, dtype=jnp.int32)
    piece_of = jnp.sum(jnp.where(owner[:, None] == slots[None, :], slots[:, None], 0), axis=0)
    my_piece = piece_of[lax.axis_index("own")]
    my_tile = my_piece * piece_rows // tile_pair
    keep = (int_mask[my_tile] * out_mask).astype(jnp.float32)
    masked_t = amplitudes * amp_mask.astype(amplitudes.dtype)[:, :, None]
    pieces = masked_t.reshape(pair_rows, own_count, piece_rows)
    ordered = jnp.stack(
        [lax.dynamic_index_in_dim(pieces, piece_of[slot], 1, keepdims=False) for slot in range(own_count)], axis=0
    )
    step_cols = min(256, col_count)
    sizes = (Z, X, Y, piece_rows, width, col_count, step_cols)
    dma = lambda *shape: pltpu.SemaphoreType.DMA(shape)
    vmem = pl.BlockSpec(memory_space=pltpu.VMEM)
    moved = pl.pallas_call(
        functools.partial(kernel, sizes),
        out_shape=jax.ShapeDtypeStruct((pairs_count, pair_rows, width), jnp.bfloat16),
        in_specs=[vmem, pl.BlockSpec(memory_space=pl.ANY), pl.BlockSpec(memory_space=pltpu.SMEM)],
        out_specs=vmem,
        scratch_shapes=[
            pltpu.VMEM((Z, X, 2, Y, pair_rows, piece_rows), jnp.bfloat16),
            pltpu.VMEM((piece_rows, width), jnp.bfloat16),
            pltpu.VMEM((2, CHUNK, tile_count, col_count), jnp.bfloat16),
            pltpu.VMEM((Z, X, 2, Y, pair_rows, width), jnp.float32),
            pltpu.VMEM((Z, X, Y, pair_rows, width), jnp.float32),
            pltpu.VMEM((Z, Y, X, pair_rows, width), jnp.float32),
            pltpu.VMEM((Z, X, pair_rows, width), jnp.bfloat16),
            dma(2), dma(own_count), dma(own_count), dma(Z), dma(Z), dma(Z, X), dma(Z, X),
            dma(Z), dma(Z), dma(Z, Y), dma(Z, Y), dma(Z, X), dma(Z, X),
        ],
        compiler_params=pltpu.CompilerParams(
            collective_id=0, has_side_effects=True, vmem_limit_bytes=60 * 1024 * 1024
        ),
        cost_estimate=pl.CostEstimate(
            flops=2 * pairs_count * own_count * pair_rows * piece_rows * width,
            bytes_accessed=2 * piece_rows * width, transcendentals=0,
        ),
    )(ordered, slab, keep)
    shaped = moved.reshape(pairs_count, pair_rows, tile_count, col_count)
    return jnp.transpose(shaped, (1, 2, 0, 3)).reshape(pair_rows, tile_count, pairs_count * col_count)


def solution(mesh):
    return jax.shard_map(
        local,
        mesh=mesh,
        in_specs=(
            P(("pairs", "own"), None, None),
            P("own", None, None, "pairs"),
            P(),
            P(("pairs", "own"), None),
            P(),
            P(),
        ),
        out_specs=P(("pairs", "own"), None, None),
        check_vma=False,
    )
```

time: 225 us -> 128 us (0.57)
  Pallas kernels: 0 us -> 111 us
  blocking collectives: 108 us -> 0 us
  local copies, waits for them, and re-layouts: 41.3 us -> 3.19 us
  waiting for transfers between devices: 34.4 us -> 0 us
  matrix products: 15 us -> 0 us
  between operations: 21.6 us -> 8.25 us
    pallas_call x0 -> x1, Pallas kernels: none -> 111 us  [local(): pl.pallas_call(functools.partial(kernel, sizes), out_shape=jax.ShapeDtype...]
    unnamed x1 -> x0, blocking collectives: 75.9 us -> none
    all_gather x1 -> x0, waiting for transfers between devices: 34.4 us -> none  [local(): lax.all_gather(mine.reshape(own_count * pair_rows, piece_rows), 'pairs',...]
    all_to_all x2 -> x0, blocking collectives: 31.9 us -> none  [the longest x1 18.9 us: local(): lax.all_to_all(rounded, 'pairs', split_axis=0, concat_axis=3, tiled=True)]
    dot_general x1 -> x0, local copies, waits for them, and re-layouts: 20.9 us -> none  [local(): jnp.dot(gathered, slab.reshape(piece_rows, tile_count * col_count), prefe...]
    unnamed x6 -> x0, local copies, waits for them, and re-layouts: 17.6 us -> none
    dot_general x1 -> x0, matrix products: 15 us -> none  [local(): jnp.dot(gathered, slab.reshape(piece_rows, tile_count * col_count), prefe...]
    reshape x0 -> x2, local copies, waits for them, and re-layouts: none -> 2.48 us  [the longest x1 1.43 us: local(): shaped = moved.reshape(pairs_count, pair_rows, tile_count, col_count)]
  transfers between devices with their start and end apart: 1 -> 0, of which waited for: 1 -> 0; matrix products, arithmetic and copies ran while one was open for 17% -> 0% of each run, Pallas kernels for 0% -> 0%
where the time goes in v1:
time: 128 us
  Pallas kernels  111 us (87%)
  between operations  8.25 us (6%)
  other arithmetic  5.21 us (4%)
  local copies, waits for them, and re-layouts  3.19 us (2%)
    pallas_call x1, Pallas kernels, local(): pl.pallas_call(functools.partial(kernel, sizes), out_shape=jax.ShapeDtype...  111 us

profile of v1, /device:TPU:0, one launch (start us, length us, event | category | flops | bytes accessed | tf_op | source)
XLA Modules:
  0.0 127.7 jit_solution(8131071089079509835)
XLA Ops:
  0.0 0.7 select_reduce_fusion
  0.7 0.7 convert_element_type.6
  1.4 0.7 fusion.3
  10.3 1.3 %fusion.2.keep_ref = f32[4]{0:T(128)} fusion(s32[4]{0:T(128)} %param.11, s32[4,4]{1,0:T(4,128)} %param.10, s32[]{:T(128)S(6)} %select_n.35), kind=kLoop, calls=%fused_computation.11 | loop fusion | flops 8 | bytes 52 | tf_op jit(solution)/shard_map/convert_element_type | solution.py:170
  11.6 1.6 %copy_multiply_fusion = bf16[16,4,4096]{2,0,1:T(8,128)(2,1)S(1)} fusion(bf16[16,4,4096]{2,1,0:T(4,128)(2,1)} %param.6, bf16[16,4]{0,1:T(4,128)(2,1)S(1)} %convert_element_type.6), kind=kLoop, calls=%fused_computation.1 | loop fusion | flops 262144 | bytes 1048704 | tf_op jit(solution)/shard_map/mul | solution.py:171
  13.3 0.9 pad_maximum_fusion.t_ref
  14.2 111.0 %shard_map.64 = bf16[8,16,2048]{2,1,0:T(8,128)(2,1)} custom-call(bf16[4,16,4096]{2,1,0:T(8,128)(2,1)} %pad_maximum_fusion.t_ref, bf16[4096,4,512]{2,1,0:T(4,128)(2,1)} %bitcast.24, f32[4]{0:T(128)} %fusion.2.keep_ref), custom_call_target="tpu_custom_call" | custom-call | flops 8589934592 | bytes 16777216 | tf_op jit(solution)/shard_map/pallas_call | solution.py:180
  125.2 1.4 %reshape.14 = bf16[8,16,4,512]{3,2,1,0:T(4,128)(2,1)S(1)} reshape(bf16[8,16,2048]{2,1,0:T(8,128)(2,1)} %shard_map.64) | data formatting | bytes 1048576 | tf_op jit(solution)/shard_map/reshape | solution.py:204
  126.6 1.0 copy.13
  (1 shorter events, 0.0 us)

commit v2 on v1

--- a/solution.py
+++ b/solution.py
@@ -19,12 +19,20 @@
     pair, own = lax.axis_index("pairs"), lax.axis_index("own")
     z, x = pair // X, pair % X
     y, c = own // 2, own % 2
+    near = jnp.minimum(z, Z - 1 - z)
+    longer = jnp.where(2 * z < Z - 1, 1, -1)
 
     def own_at(fy, fc):
         return ((y + Y + fy) % Y) * 2 + (c + 2 + fc) % 2
 
-    def pair_at(d, e):
-        return ((z + Z + d) % Z) * X + (x + X + e) % X
+    def x_at(e):
+        return (x + X + e) % X
+
+    def source(t):
+        if t == 0:
+            return z
+        both = z + (t + 1) // 2 * (1 if t % 2 else -1)
+        return jnp.where(t <= 2 * near, both, z + longer * (t - near))
 
     def remote(src, dst, send, recv, device):
         return pltpu.make_async_remote_copy(
@@ -47,31 +55,45 @@
     load(1, 1).start()
     pl.semaphore_wait(barrier, O - 1 + PAIRS - 1)
 
-    own_copies = []
+    own_copies = {}
     for f in range(1, O):
         fy, fc = f // 2, f % 2
         to = own_at(fy, fc)
-        copy = remote(t_ref.at[to], tbuf.at[0, 0, fc, fy], own_send.at[f], own_recv.at[f], {"own": to})
-        copy.start()
-        own_copies.append(copy)
-    tbuf[0, 0, 0, 0] = t_ref[own]
-    for copy in own_copies:
-        copy.wait_recv()
-
-    z_copies = {}
-    for d in range(1, Z):
-        z_copies[d] = remote(tbuf.at[0, 0], tbuf.at[d, 0], z_send.at[d], z_recv.at[d], {"pairs": pair_at(d, 0)})
-        z_copies[d].start()
-    x_copies = {}
-
-    def forward(d):
+        own_copies[f] = remote(t_ref.at[to], tbuf.at[z, 0, fy, fc], own_send.at[f], own_recv.at[f], {"own": to})
+        own_copies[f].start()
+    tbuf[z, 0, 0, 0] = t_ref[own]
+
+    def z_copy(t, h, up):
+        s = source(t)
+        to = jnp.where(up == 1, jnp.minimum(z + 1, Z - 1), jnp.maximum(z - 1, 0))
+        block = tbuf.at[s, 0, h]
+        return remote(block, block, z_send.at[t, h, up], z_recv.at[s, h], {"pairs": to * X + x})
+
+    def z_needed(t, up):
+        s = source(t)
+        if up:
+            return jnp.logical_and(s <= z, z + 1 < Z)
+        return jnp.logical_and(s >= z, z >= 1)
+
+    def x_copy(t, h, e):
+        s = source(t)
+        return remote(
+            tbuf.at[s, 0, h], tbuf.at[s, e, h], x_send.at[t, h, e], x_recv.at[t, h, e], {"pairs": z * X + x_at(e)}
+        )
+
+    def arrive(t, h):
+        if t == 0:
+            for fc in range(2):
+                if 2 * h + fc:
+                    own_copies[2 * h + fc].wait_recv()
+        else:
+            z_copy(t, h, 0).wait_recv()
+        for up in range(2):
+            @pl.when(z_needed(t, up))
+            def _():
+                z_copy(t, h, up).start()
         for e in range(1, X):
-            x_copies[d, e] = remote(
-                tbuf.at[d, 0], tbuf.at[d, e], x_send.at[d, e], x_recv.at[d, e], {"pairs": pair_at(0, e)}
-            )
-            x_copies[d, e].start()
-
-    forward(0)
+            x_copy(t, h, e).start()
 
     def flatten(first, last):
         @pl.loop(first // 2, last // 2)
@@ -86,70 +108,92 @@
                 def _():
                     load(i + 2, slot).start()
 
-    flatten(0, chunks)
-
-    c_copies, y_copies, o_copies = {}, {}, []
-
-    def multiply(d):
-        rows = tbuf.at[d]
+    c_copies, y_copies = {}, {}
+
+    def multiply(t):
+        s = source(t)
+        for e in range(1, X):
+            for h in range(Y):
+                x_copy(t, h, e).wait_recv()
 
         @pl.loop(0, N // step_cols)
         def _(n):
             at = pl.ds(pl.multiple_of(n * step_cols, step_cols), step_cols)
-            a = rows[...].reshape(X * O * 16, K)
-            product = jnp.dot(a, vbuf[:, at], preferred_element_type=jnp.float32)
+            rows = tbuf[s].reshape(X * O * 16, K)
+            product = jnp.dot(rows, vbuf[:, at], preferred_element_type=jnp.float32)
             scale = keep_ref[n * step_cols // cols]
-            part[d, :, :, :, :, at] = (product * scale).reshape(X, 2, Y, 16, step_cols)
-
-        c_copies[d] = remote(part.at[d, :, 1], core_in.at[d], c_send.at[d], c_recv.at[d], {"own": own_at(0, 1)})
-        c_copies[d].start()
-
-    def add_core(d):
-        c_copies[d].wait_recv()
+            part[t, :, :, :, :, at] = (product * scale).reshape(X, Y, 2, 16, step_cols)
+
+        c_copies[t] = remote(part.at[t, :, :, 1], core_in.at[t], c_send.at[t], c_recv.at[t], {"own": own_at(0, 1)})
+        c_copies[t].start()
+
+    def add_core(t):
+        c_copies[t].wait_recv()
+        for fy in list(range(1, Y)) + [0]:
+            for e in range(X):
+                part[t, e, fy, 0] = part[t, e, fy, 0] + core_in[t, e, fy]
+            if fy:
+                y_copies[t, fy] = remote(
+                    part.at[t, :, fy, 0], side_in.at[t, fy], y_send.at[t, fy], y_recv.at[t, fy],
+                    {"own": own_at(-fy, 0)},
+                )
+                y_copies[t, fy].start()
+
+    def o_copy(t, e):
+        return remote(
+            done.at[t, e], out_ref.at[pair], o_send.at[t, e], o_recv.at[z, e], {"pairs": source(t) * X + x_at(-e)}
+        )
+
+    def add_side(t):
+        for fy in range(1, Y):
+            y_copies[t, fy].wait_recv()
         for e in range(X):
-            for fy in range(Y):
-                part[d, e, 0, fy] = part[d, e, 0, fy] + core_in[d, e, fy]
-        for fy in range(1, Y):
-            y_copies[d, fy] = remote(
-                part.at[d, :, 0, fy], side_in.at[d, fy], y_send.at[d, fy], y_recv.at[d, fy], {"own": own_at(-fy, 0)}
-            )
-            y_copies[d, fy].start()
-
-    def add_side(d):
-        for fy in range(1, Y):
-            y_copies[d, fy].wait_recv()
-        for e in range(X):
-            total = part[d, e, 0, 0]
+            total = part[t, e, 0, 0]
             for fy in range(1, Y):
-                total = total + side_in[d, fy, e]
+                total = total + side_in[t, fy, e]
             rounded = total.astype(jnp.bfloat16)
-            if d == 0 and e == 0:
+            if t == 0 and e == 0:
                 out_ref[pair] = rounded
             else:
-                done[d, e] = rounded
-                copy = remote(done.at[d, e], out_ref.at[pair], o_send.at[d, e], o_recv.at[d, e], {"pairs": pair_at(-d, -e)})
-                copy.start()
-                o_copies.append(copy)
-
-    for d in range(Z):
-        if d + 1 < Z:
-            z_copies[d + 1].wait_recv()
-            forward(d + 1)
-        for e in range(1, X):
-            x_copies[d, e].wait_recv()
-        multiply(d)
-        if d >= 1:
-            add_core(d - 1)
-        if d >= 2:
-            add_side(d - 2)
+                done[t, e] = rounded
+                o_copy(t, e).start()
+
+    early = [(0, h) for h in range(Y)] + [(t, h) for h in range(Y) for t in range(1, min(3, Z))]
+    cuts = [chunks * k // (len(early) - 1) // 2 * 2 for k in range(len(early))]
+    for k, (t, h) in enumerate(early):
+        if k:
+            flatten(cuts[k - 1], cuts[k])
+        arrive(t, h)
+    for t in range(Z):
+        if t >= 1 and t + 2 < Z:
+            for h in range(Y):
+                arrive(t + 2, h)
+        multiply(t)
+        if t >= 1:
+            add_core(t - 1)
+        if t >= 2:
+            add_side(t - 2)
     add_core(Z - 1)
-    if Z >= 2:
-        add_side(Z - 2)
+    add_side(Z - 2)
     add_side(Z - 1)
-    for copy in o_copies:
-        copy.wait_recv()
-    for group in (own_copies, z_copies.values(), x_copies.values(), c_copies.values(), y_copies.values(), o_copies):
-        for copy in group:
+    for t in range(Z):
+        for e in range(X):
+            if t or e:
+                s = source(t)
+                remote(
+                    done.at[t, e], out_ref.at[s * X + x_at(e)], o_send.at[t, e], o_recv.at[s, e], {"pairs": s * X + x_at(e)}
+                ).wait_recv()
+                o_copy(t, e).wait_send()
+    for t in range(Z):
+        for h in range(Y):
+            for up in range(2):
+                @pl.when(z_needed(t, up))
+                def _():
+                    z_copy(t, h, up).wait_send()
+            for e in range(1, X):
+                x_copy(t, h, e).wait_send()
+    for group in (own_copies, c_copies, y_copies):
+        for copy in group.values():
             copy.wait_send()
 
 
@@ -183,14 +227,14 @@
         in_specs=[vmem, pl.BlockSpec(memory_space=pl.ANY), pl.BlockSpec(memory_space=pltpu.SMEM)],
         out_specs=vmem,
         scratch_shapes=[
-            pltpu.VMEM((Z, X, 2, Y, pair_rows, piece_rows), jnp.bfloat16),
+            pltpu.VMEM((Z, X, Y, 2, pair_rows, piece_rows), jnp.bfloat16),
             pltpu.VMEM((piece_rows, width), jnp.bfloat16),
             pltpu.VMEM((2, CHUNK, tile_count, col_count), jnp.bfloat16),
-            pltpu.VMEM((Z, X, 2, Y, pair_rows, width), jnp.float32),
+            pltpu.VMEM((Z, X, Y, 2, pair_rows, width), jnp.float32),
             pltpu.VMEM((Z, X, Y, pair_rows, width), jnp.float32),
             pltpu.VMEM((Z, Y, X, pair_rows, width), jnp.float32),
             pltpu.VMEM((Z, X, pair_rows, width), jnp.bfloat16),
-            dma(2), dma(own_count), dma(own_count), dma(Z), dma(Z), dma(Z, X), dma(Z, X),
+            dma(2), dma(own_count), dma(own_count), dma(Z, Y, 2), dma(Z, Y), dma(Z, Y, X), dma(Z, Y, X),
             dma(Z), dma(Z), dma(Z, Y), dma(Z, Y), dma(Z, X), dma(Z, X),
         ],
         compiler_params=pltpu.CompilerParams(

time: 128 us -> 99.6 us (0.78)
  Pallas kernels: 111 us -> 82.4 us
    pallas_call x1, Pallas kernels: 111 us -> 82.4 us  [local(): pl.pallas_call(functools.partial(kernel, sizes), out_shape=jax.ShapeDtype...]
where the time goes in v2:
time: 99.6 us; the launch traced here: 99.1 us
  Pallas kernels  82.4 us (83%)
  between operations  8.25 us (8%)
  other arithmetic  5.21 us (5%)
  local copies, waits for them, and re-layouts  3.19 us (3%)
    pallas_call x1, Pallas kernels, local(): pl.pallas_call(functools.partial(kernel, sizes), out_shape=jax.ShapeDtype...  82.4 us

profile of v2, /device:TPU:0, one launch (start us, length us, event | category | flops | bytes accessed | tf_op | source)
XLA Modules:
  0.0 99.1 jit_solution(7849044545439158173)
XLA Ops:
  0.0 0.7 select_reduce_fusion
  0.7 0.7 convert_element_type.6
  1.4 0.7 fusion.3
  10.3 1.3 %fusion.2.keep_ref = f32[4]{0:T(128)} fusion(s32[4]{0:T(128)} %param.11, s32[4,4]{1,0:T(4,128)} %param.10, s32[]{:T(128)S(6)} %select_n.35), kind=kLoop, calls=%fused_computation.11 | loop fusion | flops 8 | bytes 52 | tf_op jit(solution)/shard_map/convert_element_type | solution.py:214
  11.6 1.6 %copy_multiply_fusion = bf16[16,4,4096]{2,0,1:T(8,128)(2,1)S(1)} fusion(bf16[16,4,4096]{2,1,0:T(4,128)(2,1)} %param.6, bf16[16,4]{0,1:T(4,128)(2,1)S(1)} %convert_element_type.6), kind=kLoop, calls=%fused_computation.1 | loop fusion | flops 262144 | bytes 1048704 | tf_op jit(solution)/shard_map/mul | solution.py:215
  13.3 0.9 pad_maximum_fusion.t_ref
  14.2 82.4 %shard_map.64 = bf16[8,16,2048]{2,1,0:T(8,128)(2,1)} custom-call(bf16[4,16,4096]{2,1,0:T(8,128)(2,1)} %pad_maximum_fusion.t_ref, bf16[4096,4,512]{2,1,0:T(4,128)(2,1)} %bitcast.24, f32[4]{0:T(128)} %fusion.2.keep_ref), custom_call_target="tpu_custom_call" | custom-call | flops 8589934592 | bytes 16777216 | tf_op jit(solution)/shard_map/pallas_call | solution.py:224
  96.6 1.4 %reshape.14 = bf16[8,16,4,512]{3,2,1,0:T(4,128)(2,1)S(1)} reshape(bf16[8,16,2048]{2,1,0:T(8,128)(2,1)} %shard_map.64) | data formatting | bytes 1048576 | tf_op jit(solution)/shard_map/reshape | solution.py:248
  98.0 1.0 %copy.13 = bf16[8,16,1,4,512]{4,3,0,2,1:T(4,128)(2,1)} copy(bf16[8,16,1,4,512]{4,3,2,1,0:T(4,128)(2,1)S(1)} %bitcast.23) | data formatting | bytes 1048576 | tf_op jit(solution)/shard_map/reshape | solution.py:249
  (1 shorter events, 0.0 us)

commit v3 on v2

--- a/solution.py
+++ b/solution.py
@@ -121,8 +121,7 @@
             at = pl.ds(pl.multiple_of(n * step_cols, step_cols), step_cols)
             rows = tbuf[s].reshape(X * O * 16, K)
             product = jnp.dot(rows, vbuf[:, at], preferred_element_type=jnp.float32)
-            scale = keep_ref[n * step_cols // cols]
-            part[t, :, :, :, :, at] = (product * scale).reshape(X, Y, 2, 16, step_cols)
+            part[t, :, :, :, :, at] = (product * keep_ref[pl.ds(n * step_cols // cols, 1), :]).reshape(X, Y, 2, 16, step_cols)
 
         c_copies[t] = remote(part.at[t, :, :, 1], core_in.at[t], c_send.at[t], c_recv.at[t], {"own": own_at(0, 1)})
         c_copies[t].start()
@@ -165,10 +164,14 @@
             flatten(cuts[k - 1], cuts[k])
         arrive(t, h)
     for t in range(Z):
-        if t >= 1 and t + 2 < Z:
-            for h in range(Y):
-                arrive(t + 2, h)
+        if t == 0 and Z > 3:
+            arrive(3, 0)
         multiply(t)
+        if t + 3 < Z:
+            for h in range(1, Y):
+                arrive(t + 3, h)
+            if t + 4 < Z:
+                arrive(t + 4, 0)
         if t >= 1:
             add_core(t - 1)
         if t >= 2:
@@ -207,24 +210,26 @@
     X = math.isqrt(pairs_count // 2)
     Z = pairs_count // X
     Y = own_count // 2
+    place = lax.axis_index("own")
+    split = tile_pair // piece_rows
+    step_cols = min(256, col_count)
+    piece_mask = jnp.repeat(int_mask, split, axis=0)
+    mine = (owner == place)[:, None]
+    chosen = jnp.sum(jnp.where(mine, piece_mask, 0), axis=0) * out_mask
+    keep = jnp.broadcast_to(chosen.astype(jnp.float32)[:, None], (tile_count, step_cols))
+    pieces = amplitudes.reshape(pair_rows, own_count, piece_rows)
     slots = jnp.arange(own_count, dtype=jnp.int32)
-    piece_of = jnp.sum(jnp.where(owner[:, None] == slots[None, :], slots[:, None], 0), axis=0)
-    my_piece = piece_of[lax.axis_index("own")]
-    my_tile = my_piece * piece_rows // tile_pair
-    keep = (int_mask[my_tile] * out_mask).astype(jnp.float32)
-    masked_t = amplitudes * amp_mask.astype(amplitudes.dtype)[:, :, None]
-    pieces = masked_t.reshape(pair_rows, own_count, piece_rows)
-    ordered = jnp.stack(
-        [lax.dynamic_index_in_dim(pieces, piece_of[slot], 1, keepdims=False) for slot in range(own_count)], axis=0
-    )
-    step_cols = min(256, col_count)
+    used = jnp.repeat(amp_mask, split, axis=1)[None, :, :] * (owner[None, None, :] == slots[:, None, None])
+    ordered = jnp.sum(
+        jnp.where(used[..., None] != 0, pieces[None].astype(jnp.float32), 0), axis=2
+    ).astype(jnp.bfloat16)
     sizes = (Z, X, Y, piece_rows, width, col_count, step_cols)
     dma = lambda *shape: pltpu.SemaphoreType.DMA(shape)
     vmem = pl.BlockSpec(memory_space=pltpu.VMEM)
     moved = pl.pallas_call(
         functools.partial(kernel, sizes),
         out_shape=jax.ShapeDtypeStruct((pairs_count, pair_rows, width), jnp.bfloat16),
-        in_specs=[vmem, pl.BlockSpec(memory_space=pl.ANY), pl.BlockSpec(memory_space=pltpu.SMEM)],
+        in_specs=[vmem, pl.BlockSpec(memory_space=pl.ANY), vmem],
         out_specs=vmem,
         scratch_shapes=[
             pltpu.VMEM((Z, X, Y, 2, pair_rows, piece_rows), jnp.bfloat16),

time: 99.6 us -> 92.1 us (0.925)
  between operations: 8.25 us -> 0.02 us
  local copies, waits for them, and re-layouts: 3.19 us -> 4.49 us
    mul x1 -> x0, other arithmetic: 1.62 us -> none  [local(): masked_t = amplitudes * amp_mask.astype(amplitudes.dtype)[:, :, None]]
    reduce_sum x1 -> x2, other arithmetic: 0.74 us -> 2.12 us  [the longest x1 1.35 us: local(): jnp.sum(jnp.where(used[..., None] != 0, pieces[None].astype(jnp.float32),...]
    convert_element_type x0 -> x1, local copies, waits for them, and re-layouts: none -> 1.35 us  [local(): pieces[None].astype(jnp.float32)]
where the time goes in v3:
time: 92.1 us; the launch traced here: 91.6 us
  Pallas kernels  82.3 us (89%)
  other arithmetic  4.85 us (5%)
  local copies, waits for them, and re-layouts  4.49 us (5%)
    pallas_call x1, Pallas kernels, local(): pl.pallas_call(functools.partial(kernel, sizes), out_shape=jax.ShapeDtype...  82.3 us

profile of v3, /device:TPU:0, one launch (start us, length us, event | category | flops | bytes accessed | tf_op | source)
XLA Modules:
  0.0 91.6 jit_solution(10587757479247001713)
XLA Ops:
  0.0 1.3 %copy.9 = f32[16,4,4096]{2,0,1:T(8,128)S(1)} copy(bf16[16,4,4096]{2,1,0:T(4,128)(2,1)} %param.6) | data formatting | bytes 1572864 | tf_op jit(solution)/shard_map/convert_element_type | solution.py:224
  1.4 0.7 fusion
  2.0 0.8 multiply_compare_fusion
  2.8 1.4 %select_reduce_fusion.t_ref = bf16[4,16,4096]{2,1,0:T(8,128)(2,1)} fusion(f32[16,4,4096]{2,0,1:T(8,128)S(1)} %copy.9, pred[4,16,4]{1,2,0:T(4,128)(4,1)S(1)} %multiply_compare_fusion), kind=kLoop, calls=%fused_computation | loop fusion | flops 1835008 | bytes 1573120 | tf_op jit(solution)/shard_map/reduce_sum | solution.py:223
  4.1 0.7 broadcast_compare_fusion
  4.8 0.8 select_reduce_fusion.1
  5.5 0.7 multiply_convert_fusion
  6.2 0.7 broadcast_in_dim.48.keep_ref
  6.9 82.3 %shard_map.64 = bf16[8,16,2048]{2,1,0:T(8,128)(2,1)} custom-call(bf16[4,16,4096]{2,1,0:T(8,128)(2,1)} %select_reduce_fusion.t_ref, bf16[4096,4,512]{2,1,0:T(4,128)(2,1)} %bitcast.5, f32[4,256]{1,0:T(4,128)} %broadcast_in_dim.48.keep_ref), custom_call_target="tpu_custom_call" | custom-call | flops 8589934592 | bytes 16777216 | tf_op jit(solution)/shard_map/pallas_call | solution.py:229
  89.1 1.4 %reshape.37 = bf16[8,16,4,512]{3,2,1,0:T(4,128)(2,1)S(1)} reshape(bf16[8,16,2048]{2,1,0:T(8,128)(2,1)} %shard_map.64) | data formatting | bytes 1048576 | tf_op jit(solution)/shard_map/reshape | solution.py:253
  90.6 1.0 %copy.11 = bf16[8,16,1,4,512]{4,3,0,2,1:T(4,128)(2,1)} copy(bf16[8,16,1,4,512]{4,3,2,1,0:T(4,128)(2,1)S(1)} %bitcast.4) | data formatting | bytes 1048576 | tf_op jit(solution)/shard_map/reshape | solution.py:254

commit v4 on v3

--- a/solution.py
+++ b/solution.py
@@ -12,7 +12,7 @@
 CHUNK = 256
 
 
-def kernel(sizes, t_ref, v_ref, keep_ref, out_ref, tbuf, vbuf, stage, part, core_in, side_in, done,
+def kernel(sizes, t_ref, v_ref, owner_ref, int_ref, mask_ref, out_ref, tbuf, vbuf, stage, part, core_in, side_in, done,
            v_sem, own_send, own_recv, z_send, z_recv, x_send, x_recv, c_send, c_recv, y_send, y_recv, o_send, o_recv):
     Z, X, Y, K, N, cols, step_cols = sizes
     O, PAIRS = 2 * Y, Z * X
@@ -108,6 +108,12 @@
                 def _():
                     load(i + 2, slot).start()
 
+    def kept(tile):
+        entry = 0
+        for piece in range(O):
+            entry = entry + jnp.where(owner_ref[piece] == own, int_ref[piece * int_ref.shape[0] // O, tile], 0)
+        return (entry * mask_ref[tile]).astype(jnp.float32)
+
     c_copies, y_copies = {}, {}
 
     def multiply(t):
@@ -121,7 +127,7 @@
             at = pl.ds(pl.multiple_of(n * step_cols, step_cols), step_cols)
             rows = tbuf[s].reshape(X * O * 16, K)
             product = jnp.dot(rows, vbuf[:, at], preferred_element_type=jnp.float32)
-            part[t, :, :, :, :, at] = (product * keep_ref[pl.ds(n * step_cols // cols, 1), :]).reshape(X, Y, 2, 16, step_cols)
+            part[t, :, :, :, :, at] = (product * kept(n * step_cols // cols)).reshape(X, Y, 2, 16, step_cols)
 
         c_copies[t] = remote(part.at[t, :, :, 1], core_in.at[t], c_send.at[t], c_recv.at[t], {"own": own_at(0, 1)})
         c_copies[t].start()
@@ -210,13 +216,8 @@
     X = math.isqrt(pairs_count // 2)
     Z = pairs_count // X
     Y = own_count // 2
-    place = lax.axis_index("own")
     split = tile_pair // piece_rows
     step_cols = min(256, col_count)
-    piece_mask = jnp.repeat(int_mask, split, axis=0)
-    mine = (owner == place)[:, None]
-    chosen = jnp.sum(jnp.where(mine, piece_mask, 0), axis=0) * out_mask
-    keep = jnp.broadcast_to(chosen.astype(jnp.float32)[:, None], (tile_count, step_cols))
     pieces = amplitudes.reshape(pair_rows, own_count, piece_rows)
     slots = jnp.arange(own_count, dtype=jnp.int32)
     used = jnp.repeat(amp_mask, split, axis=1)[None, :, :] * (owner[None, None, :] == slots[:, None, None])
@@ -229,7 +230,7 @@
     moved = pl.pallas_call(
         functools.partial(kernel, sizes),
         out_shape=jax.ShapeDtypeStruct((pairs_count, pair_rows, width), jnp.bfloat16),
-        in_specs=[vmem, pl.BlockSpec(memory_space=pl.ANY), vmem],
+        in_specs=[vmem, pl.BlockSpec(memory_space=pl.ANY)] + [pl.BlockSpec(memory_space=pltpu.SMEM)] * 3,
         out_specs=vmem,
         scratch_shapes=[
             pltpu.VMEM((Z, X, Y, 2, pair_rows, piece_rows), jnp.bfloat16),
@@ -249,7 +250,7 @@
             flops=2 * pairs_count * own_count * pair_rows * piece_rows * width,
             bytes_accessed=2 * piece_rows * width, transcendentals=0,
         ),
-    )(ordered, slab, keep)
+    )(ordered, slab, owner, int_mask, out_mask)
     shaped = moved.reshape(pairs_count, pair_rows, tile_count, col_count)
     return jnp.transpose(shaped, (1, 2, 0, 3)).reshape(pair_rows, tile_count, pairs_count * col_count)
 

time: 92.1 us -> 89.4 us (0.971)
  other arithmetic: 4.85 us -> 2.76 us
where the time goes in v4:
time: 89.4 us; the launch traced here: 89 us
  Pallas kernels  82.4 us (92%)
  local copies, waits for them, and re-layouts  3.83 us (4%)
  other arithmetic  2.76 us (3%)
    pallas_call x1, Pallas kernels, local(): pl.pallas_call(functools.partial(kernel, sizes), out_shape=jax.ShapeDtype...  82.4 us

profile of v4, /device:TPU:0, one launch (start us, length us, event | category | flops | bytes accessed | tf_op | source)
XLA Modules:
  0.0 89.0 jit_solution(9205508337820670514)
XLA Ops:
  0.0 0.7 fusion
  0.7 0.8 multiply_compare_fusion
  1.4 1.4 %copy.9 = f32[16,4,4096]{2,0,1:T(8,128)S(1)} copy(bf16[16,4,4096]{2,1,0:T(4,128)(2,1)} %param.6) | data formatting | bytes 1572864 | tf_op jit(solution)/shard_map/convert_element_type | solution.py:225
  2.8 1.3 %select_reduce_fusion.t_ref = bf16[4,16,4096]{2,1,0:T(8,128)(2,1)} fusion(f32[16,4,4096]{2,0,1:T(8,128)S(1)} %copy.9, pred[4,16,4]{1,2,0:T(4,128)(4,1)S(1)} %multiply_compare_fusion), kind=kLoop, calls=%fused_computation | loop fusion | flops 1835008 | bytes 1573120 | tf_op jit(solution)/shard_map/reduce_sum | solution.py:224
  4.1 82.4 %shard_map.64 = bf16[8,16,2048]{2,1,0:T(8,128)(2,1)} custom-call(bf16[4,16,4096]{2,1,0:T(8,128)(2,1)} %select_reduce_fusion.t_ref, bf16[4096,4,512]{2,1,0:T(4,128)(2,1)} %bitcast.5, s32[4]{0:T(128)} %owner_ref.1, s32[4,4]{1,0:T(4,128)} %int_ref.1, s32[4]{0:T(128)} %mask_ref.1), custom_call_target="tpu_custom_call" | custom-call | flops 8589934592 | bytes 16777216 | tf_op jit(solution)/shard_map/pallas_call | solution.py:230
  86.5 1.4 %reshape.35 = bf16[8,16,4,512]{3,2,1,0:T(4,128)(2,1)S(1)} reshape(bf16[8,16,2048]{2,1,0:T(8,128)(2,1)} %shard_map.64) | data formatting | bytes 1048576 | tf_op jit(solution)/shard_map/reshape | solution.py:254
  88.0 1.0 %copy.11 = bf16[8,16,1,4,512]{4,3,0,2,1:T(4,128)(2,1)} copy(bf16[8,16,1,4,512]{4,3,2,1,0:T(4,128)(2,1)S(1)} %bitcast.4) | data formatting | bytes 1048576 | tf_op jit(solution)/shard_map/reshape | solution.py:255

commit v5 on v4

--- a/solution.py
+++ b/solution.py
@@ -170,14 +170,10 @@
             flatten(cuts[k - 1], cuts[k])
         arrive(t, h)
     for t in range(Z):
-        if t == 0 and Z > 3:
-            arrive(3, 0)
+        if t + 3 < Z:
+            for h in range(Y):
+                arrive(t + 3, h)
         multiply(t)
-        if t + 3 < Z:
-            for h in range(1, Y):
-                arrive(t + 3, h)
-            if t + 4 < Z:
-                arrive(t + 4, 0)
         if t >= 1:
             add_core(t - 1)
         if t >= 2:

time: 89.4 us -> 90.5 us (1.012)
  Pallas kernels: 82.4 us -> 83.5 us
    pallas_call x1, Pallas kernels: 82.4 us -> 83.5 us  [local(): pl.pallas_call(functools.partial(kernel, sizes), out_shape=jax.ShapeDtype...]
where the time goes in v5:
time: 90.5 us; the launch traced here: 90.1 us
  Pallas kernels  83.5 us (92%)
  local copies, waits for them, and re-layouts  3.83 us (4%)
  other arithmetic  2.76 us (3%)
    pallas_call x1, Pallas kernels, local(): pl.pallas_call(functools.partial(kernel, sizes), out_shape=jax.ShapeDtype...  83.5 us

profile of v5, /device:TPU:0, one launch (start us, length us, event | category | flops | bytes accessed | tf_op | source)
XLA Modules:
  0.0 90.1 jit_solution(6294593658933692714)
XLA Ops:
  0.0 0.7 fusion
  0.7 0.8 multiply_compare_fusion
  1.4 1.4 %copy.9 = f32[16,4,4096]{2,0,1:T(8,128)S(1)} copy(bf16[16,4,4096]{2,1,0:T(4,128)(2,1)} %param.6) | data formatting | bytes 1572864 | tf_op jit(solution)/shard_map/convert_element_type | solution.py:221
  2.8 1.3 %select_reduce_fusion.t_ref = bf16[4,16,4096]{2,1,0:T(8,128)(2,1)} fusion(f32[16,4,4096]{2,0,1:T(8,128)S(1)} %copy.9, pred[4,16,4]{1,2,0:T(4,128)(4,1)S(1)} %multiply_compare_fusion), kind=kLoop, calls=%fused_computation | loop fusion | flops 1835008 | bytes 1573120 | tf_op jit(solution)/shard_map/reduce_sum | solution.py:220
  4.1 83.5 %shard_map.64 = bf16[8,16,2048]{2,1,0:T(8,128)(2,1)} custom-call(bf16[4,16,4096]{2,1,0:T(8,128)(2,1)} %select_reduce_fusion.t_ref, bf16[4096,4,512]{2,1,0:T(4,128)(2,1)} %bitcast.5, s32[4]{0:T(128)} %owner_ref.1, s32[4,4]{1,0:T(4,128)} %int_ref.1, s32[4]{0:T(128)} %mask_ref.1), custom_call_target="tpu_custom_call" | custom-call | flops 8589934592 | bytes 16777216 | tf_op jit(solution)/shard_map/pallas_call | solution.py:226
  87.6 1.4 %reshape.35 = bf16[8,16,4,512]{3,2,1,0:T(4,128)(2,1)S(1)} reshape(bf16[8,16,2048]{2,1,0:T(8,128)(2,1)} %shard_map.64) | data formatting | bytes 1048576 | tf_op jit(solution)/shard_map/reshape | solution.py:250
  89.1 1.0 %copy.11 = bf16[8,16,1,4,512]{4,3,0,2,1:T(4,128)(2,1)} copy(bf16[8,16,1,4,512]{4,3,2,1,0:T(4,128)(2,1)S(1)} %bitcast.4) | data formatting | bytes 1048576 | tf_op jit(solution)/shard_map/reshape | solution.py:251
